TPU v7x, 32 devices: a whole 2x2x4 slice. The times are simulated.
32 devices in a mesh: dp: 8 (over z, y), mp: 4 (over x, core).
Axes of the slice: x: 2, y: 2, z: 4, core: 2. Of those that a mesh axis runs over, the one named last changes fastest.
Arguments:
- points: float32 [16384, 256], P('dp'), may hold values from -28 to 28
- residual: float32 [128, 16384], P('mp', 'dp'), may hold values from -6 to 6
- coeffs: float32 [128, 16384], P('mp', 'dp'), may hold values from -4 to 4
- block_index: int32 [512], replicated, may hold values from 0 to 16383, as said below
Outputs:
- new_residual: float32 [128, 16384], P('mp', 'dp')
- new_coeffs: float32 [128, 16384], P('mp', 'dp')
Inputs may be any that keep to these rules, and one draw needn't show every extreme that they name: `block_index`: distinct example indices; the 2048 examples of one index of dp hold at most 256 of them, and those of some index hold exactly 256.
All inputs are finite; a program needn't handle non-finite values.
Results may differ from a plain program's by a relative error of at most 0.00018.
Values sent between devices are 32-bit elements; how exact they have to be, the bound alone decides.
A program may use at most 64 MiB of HBM per device.

v0:
```python
import functools

import jax
import jax.numpy as jnp
from jax import lax
from jax.experimental import pallas as pl
from jax.experimental.pallas import tpu as pltpu
from jax.sharding import PartitionSpec as P

MESH = pl.DeviceIdType.MESH
F32 = jnp.float32
BF16 = jnp.bfloat16
HIGHEST = lax.Precision.HIGHEST
ridge_weight = 1.0
PIVOT = 128
GROUP = 8
VMEM_BYTES = 56 * 1024 * 1024


def pieces(x, count):
    out = []
    for _ in range(count):
        part = x.astype(BF16)
        out.append(part)
        x = x - part.astype(F32)
    return out


def dot(a, b, dims=((1,), (0,)), precision=None):
    return lax.dot_general(a, b, (dims, ((), ())), precision=precision, preferred_element_type=F32)


def dot3(a, b, dims=((1,), (0,))):
    a0, a1 = pieces(a, 2)
    b0, b1 = pieces(b, 2)
    return dot(a0, b0, dims) + (dot(a0, b1, dims) + dot(a1, b0, dims))


def picked_points(index_col, points, base):
    local = index_col - base
    hot = (lax.broadcasted_iota(jnp.int32, (index_col.shape[0], points.shape[0]), 1) == local).astype(BF16)
    total = None
    for part in reversed(pieces(points, 3)):
        term = dot(hot, part)
        total = term if total is None else total + term
    return total


def picked_resid(index_row, residual, base):
    local = index_row - base
    hot = (lax.broadcasted_iota(jnp.int32, (residual.shape[1], index_row.shape[1]), 0) == local).astype(BF16)
    rows = residual.shape[0]
    got = dot(jnp.concatenate(pieces(residual, 3), axis=0), hot)
    return (got[2 * rows :] + got[rows : 2 * rows]) + got[:rows]


def square_sums(points):
    squares = points * points
    sums = jnp.sum(squares.reshape(points.shape[0] // 8, 8, points.shape[1]), axis=0)
    total = sums[:, :128]
    for start in range(128, points.shape[1], 128):
        total = total + sums[:, start : start + 128]
    return total


def exchange_kernel(dp, mp, index_col, index_row, points, residual, out_points, out_resid, out_squares,
                    send, landed, share, full, squares, first_send, first_recv, square_send, square_recv,
                    second_send, second_recv, third_send, third_recv):
    me = lax.axis_index("dp")
    col = lax.axis_index("mp")
    block = index_col.shape[0]
    feat = points.shape[1]
    quarter = block // mp
    rows = quarter // dp
    out_rows = residual.shape[0]
    base = me * points.shape[0]

    barrier = pltpu.get_barrier_semaphore()
    for step in range(1, dp):
        pl.semaphore_signal(barrier, inc=1, device_id=(lax.rem(me + step, dp), col), device_id_type=MESH)
    for step in range(1, mp):
        pl.semaphore_signal(barrier, inc=1, device_id=(me, lax.rem(col + step, mp)), device_id_type=MESH)

    squares[me] = square_sums(points[...])
    got = picked_points(index_col[pl.ds(pl.multiple_of(col * quarter, quarter), quarter), :], points[...], base)
    resid = picked_resid(index_row[...], residual[...], base)
    for d in range(dp):
        send[d, :, :feat] = got[d * rows : (d + 1) * rows]
        tile, start = divmod(d * rows, out_rows)
        send[d, :, feat:] = resid[start : start + rows, tile * 128 : (tile + 1) * 128]
    pl.semaphore_wait(barrier, dp - 1 + mp - 1)

    first, norms = [], []
    for step in range(1, dp):
        peer = lax.rem(me + step, dp)
        first.append(pltpu.make_async_remote_copy(
            src_ref=send.at[peer], dst_ref=landed.at[me], send_sem=first_send.at[step], recv_sem=first_recv.at[step],
            device_id=(peer, col), device_id_type=MESH))
        first[-1].start()
        norms.append(pltpu.make_async_remote_copy(
            src_ref=squares.at[me], dst_ref=squares.at[me], send_sem=square_send.at[step],
            recv_sem=square_recv.at[step], device_id=(peer, col), device_id_type=MESH))
        norms[-1].start()
    landed[me] = send[me]
    for copy in first:
        copy.wait()
    total = landed[0]
    for d in range(1, dp):
        total = total + landed[d]
    share[...] = total
    second = []
    for step in range(1, dp):
        peer = lax.rem(me + step, dp)
        second.append(pltpu.make_async_remote_copy(
            src_ref=share, dst_ref=full.at[me], send_sem=second_send.at[step], recv_sem=second_recv.at[step],
            device_id=(peer, col), device_id_type=MESH))
        second[-1].start()
    full[me] = total
    third = []
    for step in range(dp):
        source = lax.rem(me + dp - step, dp)
        if step > 0:
            second[step - 1].wait_recv()
        place = pl.ds(pl.multiple_of(col * quarter + source * rows, rows), rows)
        out_points[place, :] = full[source, :, :feat]
        for other in range(1, mp):
            third.append(pltpu.make_async_remote_copy(
                src_ref=full.at[source, :, pl.ds(0, feat)], dst_ref=out_points.at[place, :],
                send_sem=third_send.at[step, other], recv_sem=third_recv.at[step, other],
                device_id=(me, lax.rem(col + other, mp)), device_id_type=MESH))
            third[-1].start()
    for copy in norms:
        copy.wait()
    sums = squares[0]
    for d in range(1, dp):
        sums = sums + squares[d]
    out_squares[...] = sums
    for d in range(dp):
        tile, start = divmod(d * rows, out_rows)
        out_resid[start : start + rows, tile * 128 : (tile + 1) * 128] = full[d, :, feat:]
    for copy in second:
        copy.wait_send()
    for copy in third:
        copy.wait()


def exchange(dp, mp, index_col, index_row, points, residual):
    block, feat = index_col.shape[0], points.shape[1]
    rows = block // (dp * mp)
    out_rows = residual.shape[0]
    width = feat + 128
    vmem = pl.BlockSpec(memory_space=pltpu.VMEM)
    dma = pltpu.SemaphoreType.DMA
    return pl.pallas_call(
        functools.partial(exchange_kernel, dp, mp),
        out_shape=(jax.ShapeDtypeStruct((block, feat), F32), jax.ShapeDtypeStruct((out_rows, block), F32),
                   jax.ShapeDtypeStruct((8, 128), F32)),
        in_specs=[vmem] * 4,
        out_specs=(vmem,) * 3,
        scratch_shapes=[
            pltpu.VMEM((dp, rows, width), F32), pltpu.VMEM((dp, rows, width), F32), pltpu.VMEM((rows, width), F32),
            pltpu.VMEM((dp, rows, width), F32), pltpu.VMEM((dp, 8, 128), F32),
            dma((dp,)), dma((dp,)), dma((dp,)), dma((dp,)), dma((dp,)), dma((dp,)), dma((dp, mp)), dma((dp, mp)),
        ],
        compiler_params=pltpu.CompilerParams(collective_id=0, has_side_effects=True, vmem_limit_bytes=VMEM_BYTES),
    )(index_col, index_row, points, residual)


def exchange_by_sums(dp, mp, index_col, index_row, points, residual):
    base = lax.axis_index("dp") * points.shape[0]
    local = index_col[:, 0] - base
    mine = (local >= 0) & (local < points.shape[0])
    safe = jnp.where(mine, local, 0)
    got = jnp.where(mine[:, None], points[safe], 0.0)
    resid = jnp.where(mine[None, :], residual[:, safe], 0.0)
    return tuple(lax.psum(x, "dp") for x in (got, resid, square_sums(points)))


def invert(matrix):
    size = matrix.shape[0]
    lane = lax.broadcasted_iota(jnp.int32, (size, size), 1)
    lane_group = lax.broadcasted_iota(jnp.int32, (GROUP, size), 1)
    row_group = lax.broadcasted_iota(jnp.int32, (GROUP, size), 0)
    for start in range(0, size, GROUP):
        stop = start + GROUP
        columns = [jnp.broadcast_to(matrix[:, j : j + 1], (size, size)) for j in range(start, stop)]
        small = [c[start:stop] for c in columns]
        panel = jnp.where((lane_group >= start) & (lane_group < stop),
                          (lane_group - start == row_group).astype(F32), matrix[start:stop])
        for j in range(GROUP):
            on_row = row_group == j
            scale = 1.0 / small[j][j : j + 1]
            factor = jnp.where(on_row, 0.0, small[j])
            row = panel[j : j + 1] * scale
            panel = jnp.where(on_row, row, panel) - factor * row
            for l in range(j + 1, GROUP):
                entry = small[l][j : j + 1] * scale
                small[l] = jnp.where(on_row, entry, small[l]) - factor * entry
        matrix = jnp.where((lane >= start) & (lane < stop), 0.0, matrix)
        for j in range(GROUP):
            matrix = matrix - columns[j] * panel[j : j + 1]
        parts = [matrix[:start], panel, matrix[stop:]]
        matrix = jnp.concatenate([p for p in parts if p.shape[0]], axis=0)
    return matrix


def step_kernel(examples, index_col, points, residual, coeffs, block_points, block_resid, squares,
                new_residual, new_coeffs, system, inverses, rhs):
    block, feat = block_points.shape
    count = points.shape[0]
    out_rows = residual.shape[0]
    base = lax.axis_index("dp") * count
    mean_sq = jnp.sum(squares[...]) / examples
    ones = jnp.ones((8, feat), F32)
    centers = block_points[...]
    center_sq = jnp.sum(centers * centers, axis=1, keepdims=True)
    center_sq_row = dot(ones, centers * centers, ((1,), (1,)), HIGHEST)[:1]
    inner = dot(centers, centers, ((1,), (1,)), HIGHEST)
    diagonal = lax.broadcasted_iota(jnp.int32, (block, block), 0) == lax.broadcasted_iota(jnp.int32, (block, block), 1)
    system[...] = jnp.exp(-(center_sq + center_sq_row - 2.0 * inner) / mean_sq) + jnp.where(diagonal, ridge_weight, 0.0)
    rhs[...] = block_resid[...]

    for start in range(0, block, PIVOT):
        stop = start + PIVOT
        inverse = invert(system[start:stop, start:stop])
        inverses[start:stop, :] = inverse
        if stop < block:
            right = system[start:stop, stop:]
            scaled = dot(inverse, right, precision=HIGHEST)
            system[stop:, stop:] = system[stop:, stop:] - dot(right, scaled, ((0,), (0,)), HIGHEST)
            rhs[:, stop:] = rhs[:, stop:] - dot(rhs[:, start:stop], scaled, precision=HIGHEST)
    for start in reversed(range(0, block, PIVOT)):
        stop = start + PIVOT
        now = rhs[:, start:stop]
        if stop < block:
            now = now - dot(rhs[:, stop:], system[start:stop, stop:], ((1,), (1,)), HIGHEST)
        rhs[:, start:stop] = dot(now, inverses[start:stop, :], precision=HIGHEST)

    high, mid, low = pieces(rhs[...], 3)
    stack3 = jnp.concatenate([high, mid, low], axis=0)
    stack2 = jnp.concatenate([high, mid], axis=0)
    tile = 256

    @pl.loop(0, count // tile)
    def _(i):
        here = pl.ds(pl.multiple_of(i * tile, tile), tile)
        some = points[here, :]
        some_sq = dot(ones, some * some, ((1,), (1,)), HIGHEST)[:1]
        inner = dot(centers, some, ((1,), (1,)), HIGHEST)
        weights = jnp.exp(-(center_sq + some_sq - 2.0 * inner) / mean_sq)
        w0, w1 = pieces(weights, 2)
        main = dot(stack2, w0)
        change = main[:out_rows] + (main[out_rows:] + dot(high, w1))
        local = index_col[...] - (base + i * tile)
        hot = (lax.broadcasted_iota(jnp.int32, (block, tile), 1) == local).astype(BF16)
        placed = dot(stack3, hot)
        added = (placed[2 * out_rows :] + placed[out_rows : 2 * out_rows]) + placed[:out_rows]
        new_residual[:, here] = (residual[:, here] - change) - ridge_weight * added
        new_coeffs[:, here] = coeffs[:, here] + added


def step(examples, index_col, points, residual, coeffs, block_points, block_resid, squares):
    block = block_points.shape[0]
    vmem = pl.BlockSpec(memory_space=pltpu.VMEM)
    return pl.pallas_call(
        functools.partial(step_kernel, examples),
        out_shape=(jax.ShapeDtypeStruct(residual.shape, F32), jax.ShapeDtypeStruct(coeffs.shape, F32)),
        in_specs=[vmem] * 7,
        out_specs=(vmem,) * 2,
        scratch_shapes=[pltpu.VMEM((block, block), F32), pltpu.VMEM((block, PIVOT), F32),
                        pltpu.VMEM(residual.shape[:1] + (block,), F32)],
        compiler_params=pltpu.CompilerParams(vmem_limit_bytes=VMEM_BYTES),
    )(index_col, points, residual, coeffs, block_points, block_resid, squares)


def solution(mesh):
    dp, mp = mesh.shape["dp"], mesh.shape["mp"]

    def on_device(points, residual, coeffs, block_index):
        index_col, index_row = block_index[:, None], block_index[None, :]
        block, out_rows = block_index.shape[0], residual.shape[0]
        rows = block // (dp * mp)
        fits = rows % 8 == 0 and out_rows % rows == 0 and rows * dp * mp == block and out_rows * block == dp * rows * 128
        gathered = (exchange if fits else exchange_by_sums)(dp, mp, index_col, index_row, points, residual)
        return step(points.shape[0] * dp, index_col, points, residual, coeffs, *gathered)

    return jax.shard_map(
        on_device,
        mesh=mesh,
        in_specs=(P("dp", None), P("mp", "dp"), P("mp", "dp"), P()),
        out_specs=(P("mp", "dp"), P("mp", "dp")),
        check_vma=False,
    )
```

profile of v0, /device:TPU:0, one launch (start us, length us, event | category | flops | bytes accessed | tf_op | source)
XLA Modules:
  0.0 63.6 jit_solution(15156790309796736033)
XLA Ops:
  0.6 1.5 %copy.7.index_col = s32[512,1]{1,0:T(8,128)} copy(s32[512,1]{0,1:T(1,128)} %bitcast.2) | data formatting | bytes 4096 | tf_op jit(solution)/shard_map/broadcast_in_dim | solution.py:280
  2.2 25.9 %shard_map.59 = (f32[512,256]{1,0:T(8,128)}, f32[32,512]{1,0:T(8,128)}, f32[8,128]{1,0:T(8,128)}) custom-call(s32[512,1]{1,0:T(8,128)} %copy.7.index_col, s32[1,512]{1,0:T(1,128)} %bitcast.3, f32[2048,256]{1,0:T(8,128)} %points.3, f32[32,2048]{1,0:T(8,128)} %residual.3), custom_call_target="tpu_custom_call" | custom-call | tf_op jit(solution)/shard_map/pallas_call | solution.py:154
  28.0 35.5 %shard_map.60 = (f32[32,2048]{1,0:T(8,128)}, f32[32,2048]{1,0:T(8,128)}) custom-call(s32[512,1]{1,0:T(8,128)} %copy.7.index_col, f32[2048,256]{1,0:T(8,128)} %points.3, f32[32,2048]{1,0:T(8,128)} %residual.3, f32[32,2048]{1,0:T(8,128)} %coeffs.1, f32[512,256]{1,0:T(8,128)} %get-tuple-element.5.block_points, f32[32,512]{1,0:T(8,128)} %get-tuple-element.6.block_resid, ...), custom_call_target="tpu_custom_call" | custom-call | tf_op jit(solution)/shard_map/pallas_call | solution.py:265
where the time goes:
time: 63.7 us; the launch traced here: 63.6 us
  Pallas kernels  61.4 us (96%)
  local copies, waits for them, and re-layouts  1.53 us (2%)
  between operations  0.64 us (1%)
    pallas_call x1, Pallas kernels, step(): pl.pallas_call(functools.partial(step_kernel, examples), out_shape=(jax.S...  35.5 us
    pallas_call x1, Pallas kernels, exchange(): pl.pallas_call(functools.partial(exchange_kernel, dp, mp), out_shape=(jax...  25.9 us
    broadcast_in_dim x1, local copies, waits for them, and re-layouts, on_device(): index_col, index_row = (block_index[:, None], block_index[None, :])  1.53 us

commit v1 on v0

v1 whole, which is shorter than its diff:
```python
import functools

import jax
import jax.numpy as jnp
from jax import lax
from jax.experimental import pallas as pl
from jax.experimental.pallas import tpu as pltpu
from jax.sharding import PartitionSpec as P

MESH = pl.DeviceIdType.MESH
F32 = jnp.float32
BF16 = jnp.bfloat16
HIGHEST = lax.Precision.HIGHEST
ridge_weight = 1.0
PIVOT = 128
GROUP = 8
VMEM_BYTES = 56 * 1024 * 1024


def pieces(x, count):
    out = []
    for _ in range(count):
        part = x.astype(BF16)
        out.append(part)
        x = x - part.astype(F32)
    return out


def dot(a, b, dims=((1,), (0,)), precision=None):
    return lax.dot_general(a, b, (dims, ((), ())), precision=precision, preferred_element_type=F32)


def dot3(a, b, dims=((1,), (0,))):
    a0, a1 = pieces(a, 2)
    b0, b1 = pieces(b, 2)
    return dot(a0, b0, dims) + (dot(a0, b1, dims) + dot(a1, b0, dims))


def picked_points(index_col, points, base):
    local = index_col - base
    hot = (lax.broadcasted_iota(jnp.int32, (index_col.shape[0], points.shape[0]), 1) == local).astype(BF16)
    total = None
    for part in reversed(pieces(points, 3)):
        term = dot(hot, part)
        total = term if total is None else total + term
    return total


def picked_resid(index_row, residual, base):
    local = index_row - base
    hot = (lax.broadcasted_iota(jnp.int32, (residual.shape[1], index_row.shape[1]), 0) == local).astype(BF16)
    rows = residual.shape[0]
    got = dot(jnp.concatenate(pieces(residual, 3), axis=0), hot)
    return (got[2 * rows :] + got[rows : 2 * rows]) + got[:rows]


def square_sums(points):
    squares = points * points
    sums = jnp.sum(squares.reshape(points.shape[0] // 8, 8, points.shape[1]), axis=0)
    total = sums[:, :128]
    for start in range(128, points.shape[1], 128):
        total = total + sums[:, start : start + 128]
    return total


def exchange_kernel(dp, mp, index_row, points, residual, out_points, out_resid, out_squares,
                    send, landed, share, full, squares, first_send, first_recv, square_send, square_recv,
                    second_send, second_recv, third_send, third_recv):
    me = lax.axis_index("dp")
    col = lax.axis_index("mp")
    block = index_row.shape[1]
    feat = points.shape[1]
    quarter = block // mp
    rows = quarter // dp
    out_rows = residual.shape[0]
    base = me * points.shape[0]

    barrier = pltpu.get_barrier_semaphore()
    for step in range(1, dp):
        pl.semaphore_signal(barrier, inc=1, device_id=(lax.rem(me + step, dp), col), device_id_type=MESH)
    near, far = col + 1 - 2 * lax.rem(col, 2), lax.rem(col + 2, mp)
    for other in (near, far):
        pl.semaphore_signal(barrier, inc=1, device_id=(me, other), device_id_type=MESH)

    squares[me] = square_sums(points[...])
    own = index_row[:, pl.ds(pl.multiple_of(col * quarter, quarter), quarter)]
    own = jnp.transpose(jnp.broadcast_to(own, (128, quarter)))[:, :1]
    got = picked_points(own, points[...], base)
    resid = picked_resid(index_row[...], residual[...], base)
    for d in range(dp):
        send[d, :, :feat] = got[d * rows : (d + 1) * rows]
        tile, start = divmod(d * rows, out_rows)
        send[d, :, feat:] = resid[start : start + rows, tile * 128 : (tile + 1) * 128]
    pl.semaphore_wait(barrier, dp - 1 + 2)

    first, norms = [], []
    for step in range(1, dp):
        peer = lax.rem(me + step, dp)
        first.append(pltpu.make_async_remote_copy(
            src_ref=send.at[peer], dst_ref=landed.at[me], send_sem=first_send.at[step], recv_sem=first_recv.at[step],
            device_id=(peer, col), device_id_type=MESH))
        first[-1].start()
        norms.append(pltpu.make_async_remote_copy(
            src_ref=squares.at[me], dst_ref=squares.at[me], send_sem=square_send.at[step],
            recv_sem=square_recv.at[step], device_id=(peer, col), device_id_type=MESH))
        norms[-1].start()
    landed[me] = send[me]
    for copy in first:
        copy.wait()
    total = landed[0]
    for d in range(1, dp):
        total = total + landed[d]
    share[...] = total
    second = []
    for step in range(1, dp):
        peer = lax.rem(me + step, dp)
        second.append(pltpu.make_async_remote_copy(
            src_ref=share, dst_ref=full.at[me], send_sem=second_send.at[step], recv_sem=second_recv.at[step],
            device_id=(peer, col), device_id_type=MESH))
        second[-1].start()
    full[me] = total
    third = []
    for step in range(dp):
        source = lax.rem(me + dp - step, dp)
        if step > 0:
            second[step - 1].wait_recv()
        place = pl.ds(pl.multiple_of(col * quarter + source * rows, rows), rows)
        out_points[place, :] = full[source, :, :feat]
        for kind, other in enumerate((far, near)):
            third.append(pltpu.make_async_remote_copy(
                src_ref=full.at[source, :, pl.ds(0, feat)], dst_ref=out_points.at[place, :],
                send_sem=third_send.at[step, kind], recv_sem=third_recv.at[step, kind],
                device_id=(me, other), device_id_type=MESH))
            third[-1].start()
    fourth = []
    for step in range(dp):
        source = lax.rem(me + dp - step, dp)
        third[2 * step].wait_recv()
        place = pl.ds(pl.multiple_of(far * quarter + source * rows, rows), rows)
        fourth.append(pltpu.make_async_remote_copy(
            src_ref=out_points.at[place, :], dst_ref=out_points.at[place, :],
            send_sem=third_send.at[step, 2], recv_sem=third_recv.at[step, 2],
            device_id=(me, near), device_id_type=MESH))
        fourth[-1].start()
    for copy in norms:
        copy.wait()
    sums = squares[0]
    for d in range(1, dp):
        sums = sums + squares[d]
    out_squares[...] = sums
    for d in range(dp):
        tile, start = divmod(d * rows, out_rows)
        out_resid[start : start + rows, tile * 128 : (tile + 1) * 128] = full[d, :, feat:]
    for copy in second:
        copy.wait_send()
    for step in range(dp):
        third[2 * step].wait_send()
        third[2 * step + 1].wait()
        fourth[step].wait()


def exchange(dp, mp, index_row, points, residual):
    block, feat = index_row.shape[1], points.shape[1]
    rows = block // (dp * mp)
    out_rows = residual.shape[0]
    width = feat + 128
    vmem = pl.BlockSpec(memory_space=pltpu.VMEM)
    dma = pltpu.SemaphoreType.DMA
    return pl.pallas_call(
        functools.partial(exchange_kernel, dp, mp),
        out_shape=(jax.ShapeDtypeStruct((block, feat), F32), jax.ShapeDtypeStruct((out_rows, block), F32),
                   jax.ShapeDtypeStruct((8, 128), F32)),
        in_specs=[vmem] * 3,
        out_specs=(vmem,) * 3,
        scratch_shapes=[
            pltpu.VMEM((dp, rows, width), F32), pltpu.VMEM((dp, rows, width), F32), pltpu.VMEM((rows, width), F32),
            pltpu.VMEM((dp, rows, width), F32), pltpu.VMEM((dp, 8, 128), F32),
            dma((dp,)), dma((dp,)), dma((dp,)), dma((dp,)), dma((dp,)), dma((dp,)), dma((dp, 3)), dma((dp, 3)),
        ],
        compiler_params=pltpu.CompilerParams(collective_id=0, has_side_effects=True, vmem_limit_bytes=VMEM_BYTES),
    )(index_row, points, residual)


def exchange_by_sums(dp, mp, index_row, points, residual):
    base = lax.axis_index("dp") * points.shape[0]
    local = index_row[0] - base
    mine = (local >= 0) & (local < points.shape[0])
    safe = jnp.where(mine, local, 0)
    got = jnp.where(mine[:, None], points[safe], 0.0)
    resid = jnp.where(mine[None, :], residual[:, safe], 0.0)
    return tuple(lax.psum(x, "dp") for x in (got, resid, square_sums(points)))


def invert(matrix, beside):
    size = matrix.shape[0]
    lane = lax.broadcasted_iota(jnp.int32, (size, size), 1)
    lane_group = lax.broadcasted_iota(jnp.int32, (GROUP, size), 1)
    row_group = lax.broadcasted_iota(jnp.int32, (GROUP, size), 0)
    for start in range(0, size, GROUP):
        stop = start + GROUP
        columns = [jnp.broadcast_to(matrix[:, j : j + 1], (size, size)) for j in range(start, stop)]
        small = [c[start:stop] for c in columns]
        panel = jnp.where((lane_group >= start) & (lane_group < stop),
                          (lane_group - start == row_group).astype(F32), matrix[start:stop])
        for j in range(0, GROUP, 2):
            k = j + 1
            on_j, on_k = row_group == j, row_group == k
            p, q, r = small[j][j : j + 1], small[j][k : k + 1], small[k][k : k + 1]
            scale = 1.0 / (p * r - q * q)
            low, cross, high = r * scale, q * scale, p * scale
            left = jnp.where(on_j, -1.0, jnp.where(on_k, 0.0, small[j]))
            right = jnp.where(on_k, -1.0, jnp.where(on_j, 0.0, small[k]))
            pivots = on_j | on_k

            def reduced(x):
                x0, x1 = x[j : j + 1], x[k : k + 1]
                y0, y1 = x0 * low - x1 * cross, x1 * high - x0 * cross
                return jnp.where(pivots, 0.0, x) - left * y0 - right * y1

            for l in range(j + 2, GROUP):
                small[l] = reduced(small[l])
            panel = reduced(panel)
        beside(start // GROUP)
        matrix = jnp.where((lane >= start) & (lane < stop), 0.0, matrix)
        for j in range(GROUP):
            matrix = matrix - columns[j] * panel[j : j + 1]
        parts = [matrix[:start], panel, matrix[stop:]]
        matrix = jnp.concatenate([p for p in parts if p.shape[0]], axis=0)
    return matrix


def step_kernel(examples, index_row, points, residual, coeffs, block_points, block_resid, squares,
                new_residual, new_coeffs, system, weights0, weights1, index_col):
    block, feat = block_points.shape
    count = points.shape[0]
    out_rows = residual.shape[0]
    base = lax.axis_index("dp") * count
    inverse_mean = examples / jnp.sum(squares[...])
    ones = jnp.ones((8, feat), F32)
    centers = block_points[...]
    center_sq = jnp.sum(centers * centers, axis=1, keepdims=True)
    center_sq_row = dot(ones, centers * centers, ((1,), (1,)), HIGHEST)[:1]
    inner = dot(centers, centers, ((1,), (1,)), HIGHEST)
    diagonal = lax.broadcasted_iota(jnp.int32, (block, block), 0) == lax.broadcasted_iota(jnp.int32, (block, block), 1)
    system[:block, :] = (jnp.exp(-(center_sq + center_sq_row - 2.0 * inner) * inverse_mean)
                         + jnp.where(diagonal, ridge_weight, 0.0))
    system[block:, :] = block_resid[...]
    index_col[...] = jnp.transpose(jnp.broadcast_to(index_row[...], (128, block)))

    groups = PIVOT // GROUP
    strips = block // PIVOT
    some_rows = count // (strips * (groups // strips))
    lane = lax.broadcasted_iota(jnp.int32, (PIVOT, block), 1)
    lane_all = lax.broadcasted_iota(jnp.int32, (block + out_rows, block), 1)

    @pl.loop(0, strips)
    def _(step):
        here = pl.ds(pl.multiple_of(step * PIVOT, PIVOT), PIVOT)
        held = {}

        def beside(n):
            strip = n % strips
            first = step * (groups // strips) + n // strips
            there = pl.ds(pl.multiple_of(first * some_rows, some_rows), some_rows)
            some = points[there, :]
            if strip == 0:
                held["sq"] = dot(ones, some * some, ((1,), (1,)), HIGHEST)[:1]
            rows = slice(strip * PIVOT, (strip + 1) * PIVOT)
            inner = dot(block_points[rows, :], some, ((1,), (1,)), HIGHEST)
            weights = jnp.exp(-(center_sq[rows] + held["sq"] - 2.0 * inner) * inverse_mean)
            w0, w1 = pieces(weights, 2)
            weights0[rows, there] = w0
            weights1[rows, there] = w1

        inverse = invert(system[here, here], beside)
        inside = (lane >= step * PIVOT) & (lane < (step + 1) * PIVOT)
        scaled = dot(inverse, system[here, :], precision=HIGHEST)
        scaled = jnp.where(inside, -jnp.concatenate([inverse] * strips, axis=1), scaled)
        left = system[:, here]
        inside_all = (lane_all >= step * PIVOT) & (lane_all < (step + 1) * PIVOT)
        system[...] = jnp.where(inside_all, 0.0, system[...]) - dot(left, scaled, precision=HIGHEST)

    high, mid, low = pieces(system[block:, :], 3)
    stack3 = jnp.concatenate([high, mid, low], axis=0)
    stack2 = jnp.concatenate([high, mid], axis=0)
    tile = 512

    @pl.loop(0, count // tile)
    def _(i):
        here = pl.ds(pl.multiple_of(i * tile, tile), tile)
        main = dot(stack2, weights0[:, here])
        change = main[:out_rows] + (main[out_rows:] + dot(high, weights1[:, here]))
        local = jnp.concatenate([index_col[...]] * (tile // 128), axis=1) - (base + i * tile)
        hot = (lax.broadcasted_iota(jnp.int32, (block, tile), 1) == local).astype(BF16)
        placed = dot(stack3, hot)
        added = (placed[2 * out_rows :] + placed[out_rows : 2 * out_rows]) + placed[:out_rows]
        new_residual[:, here] = (residual[:, here] - change) - ridge_weight * added
        new_coeffs[:, here] = coeffs[:, here] + added


def step(examples, index_row, points, residual, coeffs, block_points, block_resid, squares):
    block = block_points.shape[0]
    vmem = pl.BlockSpec(memory_space=pltpu.VMEM)
    return pl.pallas_call(
        functools.partial(step_kernel, examples),
        out_shape=(jax.ShapeDtypeStruct(residual.shape, F32), jax.ShapeDtypeStruct(coeffs.shape, F32)),
        in_specs=[vmem] * 7,
        out_specs=(vmem,) * 2,
        scratch_shapes=[pltpu.VMEM((block + residual.shape[0], block), F32),
                        pltpu.VMEM((block, points.shape[0]), BF16), pltpu.VMEM((block, points.shape[0]), BF16),
                        pltpu.VMEM((block, 128), jnp.int32)],
        compiler_params=pltpu.CompilerParams(vmem_limit_bytes=VMEM_BYTES),
    )(index_row, points, residual, coeffs, block_points, block_resid, squares)


def solution(mesh):
    dp, mp = mesh.shape["dp"], mesh.shape["mp"]

    def on_device(points, residual, coeffs, block_index):
        index_row = block_index[None, :]
        block, out_rows = block_index.shape[0], residual.shape[0]
        rows = block // (dp * mp)
        fits = mp == 4 and block // mp == 128 and rows % 8 == 0 and out_rows % rows == 0 and rows * dp * mp == block and out_rows * block == dp * rows * 128
        gathered = (exchange if fits else exchange_by_sums)(dp, mp, index_row, points, residual)
        return step(points.shape[0] * dp, index_row, points, residual, coeffs, *gathered)

    return jax.shard_map(
        on_device,
        mesh=mesh,
        in_specs=(P("dp", None), P("mp", "dp"), P("mp", "dp"), P()),
        out_specs=(P("mp", "dp"), P("mp", "dp")),
        check_vma=False,
    )
```

time: 63.7 us -> 57.7 us (0.906)
  Pallas kernels: 61.4 us -> 57 us
  local copies, waits for them, and re-layouts: 1.53 us -> 0 us
    pallas_call x1, Pallas kernels: 35.5 us -> 31.6 us  [step(): pl.pallas_call(functools.partial(step_kernel, examples), out_shape=(jax.S...]
    broadcast_in_dim x1 -> x0, local copies, waits for them, and re-layouts: 1.53 us -> none  [on_device(): index_col, index_row = (block_index[:, None], block_index[None, :])]
where the time goes in v1:
time: 57.7 us; the launch traced here: 57.6 us
  Pallas kernels  57 us (99%)
  between operations  0.64 us (1%)
    pallas_call x1, Pallas kernels, step(): pl.pallas_call(functools.partial(step_kernel, examples), out_shape=(jax.S...  31.6 us
    pallas_call x1, Pallas kernels, exchange(): pl.pallas_call(functools.partial(exchange_kernel, dp, mp), out_shape=(jax...  25.4 us

profile of v1, /device:TPU:0, one launch (start us, length us, event | category | flops | bytes accessed | tf_op | source)
XLA Modules:
  0.0 57.6 jit_solution(15286794443319672052)
XLA Ops:
  0.6 25.4 %shard_map.59 = (f32[512,256]{1,0:T(8,128)}, f32[32,512]{1,0:T(8,128)}, f32[8,128]{1,0:T(8,128)}) custom-call(s32[1,512]{1,0:T(1,128)} %bitcast.1, f32[2048,256]{1,0:T(8,128)} %points.3, f32[32,2048]{1,0:T(8,128)} %residual.3), custom_call_target="tpu_custom_call" | custom-call | tf_op jit(solution)/shard_map/pallas_call | solution.py:169
  26.0 31.6 %shard_map.60 = (f32[32,2048]{1,0:T(8,128)}, f32[32,2048]{1,0:T(8,128)}) custom-call(s32[1,512]{1,0:T(1,128)} %bitcast.2, f32[2048,256]{1,0:T(8,128)} %points.3, f32[32,2048]{1,0:T(8,128)} %residual.3, f32[32,2048]{1,0:T(8,128)} %coeffs.1, f32[512,256]{1,0:T(8,128)} %get-tuple-element.5.block_points, f32[32,512]{1,0:T(8,128)} %get-tuple-element.6.block_resid, ...), custom_call_target="tpu_custom_call" | custom-call | tf_op jit(solution)/shard_map/pallas_call | solution.py:304

commit v2 on v1

--- a/solution.py
+++ b/solution.py
@@ -198,8 +198,10 @@
     row_group = lax.broadcasted_iota(jnp.int32, (GROUP, size), 0)
     for start in range(0, size, GROUP):
         stop = start + GROUP
-        columns = [jnp.broadcast_to(matrix[:, j : j + 1], (size, size)) for j in range(start, stop)]
-        small = [c[start:stop] for c in columns]
+        small = [jnp.broadcast_to(matrix[start:stop, j : j + 1], (GROUP, size)) for j in range(start, stop)]
+        own = jnp.where(lane_group < start, -matrix[start:stop], matrix[start:stop])
+        c0, c1, c2 = [p.astype(F32) for p in pieces(own, 3)]
+        side = jnp.concatenate([c0, c0, c0, c1, c1, c2], axis=0).astype(BF16)
         panel = jnp.where((lane_group >= start) & (lane_group < stop),
                           (lane_group - start == row_group).astype(F32), matrix[start:stop])
         for j in range(0, GROUP, 2):
@@ -221,10 +223,16 @@
                 small[l] = reduced(small[l])
             panel = reduced(panel)
         beside(start // GROUP)
-        matrix = jnp.where((lane >= start) & (lane < stop), 0.0, matrix)
-        for j in range(GROUP):
-            matrix = matrix - columns[j] * panel[j : j + 1]
-        parts = [matrix[:start], panel, matrix[stop:]]
+        ahead = None
+        if stop < size:
+            old = matrix[stop : stop + GROUP]
+            ahead = jnp.where((lane_group >= start) & (lane_group < stop), 0.0, old)
+            for j in range(GROUP):
+                ahead = ahead - jnp.broadcast_to(old[:, start + j : start + j + 1], (GROUP, size)) * panel[j : j + 1]
+        zeroed = jnp.where((lane >= start) & (lane < stop), 0.0, matrix)
+        r0, r1, r2 = [p.astype(F32) for p in pieces(panel, 3)]
+        matrix = zeroed - dot(side, jnp.concatenate([r0, r1, r2, r0, r1, r0], axis=0).astype(BF16), ((0,), (0,)))
+        parts = [matrix[:start], panel] + ([] if ahead is None else [ahead, matrix[stop + GROUP :]])
         matrix = jnp.concatenate([p for p in parts if p.shape[0]], axis=0)
     return matrix
 

time: 57.7 us -> 52.3 us (0.906)
  Pallas kernels: 57 us -> 51.5 us
    pallas_call x1, Pallas kernels: 31.6 us -> 26.1 us  [step(): pl.pallas_call(functools.partial(step_kernel, examples), out_shape=(jax.S...]
where the time goes in v2:
time: 52.3 us; the launch traced here: 52.1 us
  Pallas kernels  51.5 us (98%)
  between operations  0.64 us (1%)
    pallas_call x1, Pallas kernels, step(): pl.pallas_call(functools.partial(step_kernel, examples), out_shape=(jax.S...  26.1 us
    pallas_call x1, Pallas kernels, exchange(): pl.pallas_call(functools.partial(exchange_kernel, dp, mp), out_shape=(jax...  25.4 us

profile of v2, /device:TPU:0, one launch (start us, length us, event | category | flops | bytes accessed | tf_op | source)
XLA Modules:
  0.0 52.1 jit_solution(1135573245913509542)
XLA Ops:
  0.6 25.4 %shard_map.59 = (f32[512,256]{1,0:T(8,128)}, f32[32,512]{1,0:T(8,128)}, f32[8,128]{1,0:T(8,128)}) custom-call(s32[1,512]{1,0:T(1,128)} %bitcast.1, f32[2048,256]{1,0:T(8,128)} %points.3, f32[32,2048]{1,0:T(8,128)} %residual.3), custom_call_target="tpu_custom_call" | custom-call | tf_op jit(solution)/shard_map/pallas_call | solution.py:169
  26.0 26.1 %shard_map.60 = (f32[32,2048]{1,0:T(8,128)}, f32[32,2048]{1,0:T(8,128)}) custom-call(s32[1,512]{1,0:T(1,128)} %bitcast.2, f32[2048,256]{1,0:T(8,128)} %points.3, f32[32,2048]{1,0:T(8,128)} %residual.3, f32[32,2048]{1,0:T(8,128)} %coeffs.1, f32[512,256]{1,0:T(8,128)} %get-tuple-element.5.block_points, f32[32,512]{1,0:T(8,128)} %get-tuple-element.6.block_resid, ...), custom_call_target="tpu_custom_call" | custom-call | tf_op jit(solution)/shard_map/pallas_call | solution.py:312
